TPU v7x, 256 devices: a whole 4x4x8 slice. The times are simulated.
256 devices in a mesh: pool: 8 (over z_hi, core), tp: 32 (over x, z_lo, y).
Axes of the slice: x: 4, y: 4, z: 8 (z_hi: 4, z_lo: 2; z = z_hi * 2 + z_lo), core: 2. Of those that a mesh axis runs over, the one named last changes fastest.
Arguments:
- hidden: bfloat16 [2048, 8192], P(('pool', 'tp'))
- norm_gain: float32 [8192], replicated, may hold values from 0.1 to 1.9
- start_positions: int32 [32], P('pool'), may hold values from 256 to 4095
- draft_lengths: int32 [32], P('pool'), may hold values from 1 to 64
- query_weight: bfloat16 [8192, 8192], P(None, 'tp'), may hold values from -0.0625 to 0.0625
- w_keyvalue: bfloat16 [32, 8192, 256], P('tp'), as said below
- output_weight: bfloat16 [8192, 8192], P('tp'), may hold values from -0.0625 to 0.0625
- kv_cache: bfloat16 [32, 256, 32, 256], P('pool', None, 'tp'), as said below
- a_query: bfloat16 [8192, 64], P(('tp', 'pool')), may hold values from -0.0625 to 0.0625
- b_query: bfloat16 [64, 8192], P(None, ('tp', 'pool')), may hold values from -0.75 to 0.75
- a_key: bfloat16 [8192, 64], P(('tp', 'pool')), may hold values from -0.0625 to 0.0625
- b_key: bfloat16 [64, 1024], P(None, ('tp', 'pool')), may hold values from -0.75 to 0.75
- a_value: bfloat16 [8192, 64], P(('tp', 'pool')), may hold values from -0.0625 to 0.0625
- b_value: bfloat16 [64, 1024], P(None, ('tp', 'pool')), may hold values from -0.75 to 0.75
- a_out: bfloat16 [8192, 64], P(('tp', 'pool')), may hold values from -0.0625 to 0.0625
- b_out: bfloat16 [64, 8192], P(None, ('tp', 'pool')), may hold values from -0.75 to 0.75
Outputs:
- updated: bfloat16 [2048, 8192], P(('pool', 'tp'))
Inputs may be any that keep to these rules, and one draw needn't show every extreme that they name: `w_keyvalue`: blocks t and u along the first dimension are equal when t // 4 == u // 4; block t holds the key columns (first 128) and value columns of key-value head t // 4. `kv_cache`: entries t and u along the third dimension are equal when t // 4 == u // 4; the first 128 entries are the key, the rest the value of key-value head t // 4.
All inputs are finite; a program needn't handle non-finite values.
Results may differ from a plain program's by a relative error of at most 0.02.
Values may be sent and summed in bfloat16 or wider, within the bound.
No kernel may reach another device: no remote copies, remote signals or barrier semaphores. Data moves between devices by JAX's collectives and lax.ppermute only.
A program may use at most 128 MiB of HBM per device.

v0:
```python
import math

import jax
import jax.numpy as jnp
from jax import lax
from jax.sharding import PartitionSpec as P

KV_HEADS = 8
VERIFY = 64


adapter_scale = 1.0
rope_base = 1000000.0
norm_eps = 1e-06


def rotate(values, places):
    half_dim = values.shape[-1] // 2
    freqs = jnp.exp(
        jnp.arange(half_dim, dtype=jnp.float32) * (-2.0 * math.log(rope_base) / values.shape[-1])
    )
    angles = places.astype(jnp.float32)[:, None] * freqs[None, :]
    cosine = jnp.cos(angles)[:, None, :]
    sine = jnp.sin(angles)[:, None, :]
    first = values[..., :half_dim]
    second = values[..., half_dim:]
    return jnp.concatenate(
        [first * cosine - second * sine, second * cosine + first * sine], axis=-1
    )


def highest_dot(left, right):
    return jnp.dot(left, right, precision=lax.Precision.HIGHEST)


def shards(
    hidden,
    norm_gain,
    start_positions,
    draft_lengths,
    query_weight,
    w_keyvalue,
    output_weight,
    kv_cache,
    a_query,
    b_query,
    a_key,
    b_key,
    a_value,
    b_value,
    a_out,
    b_out,
):
    shard_count = lax.axis_size("tp")
    shard_index = lax.axis_index("tp")
    head_dim = w_keyvalue.shape[2] // 2
    query_width = query_weight.shape[1]
    heads_here = query_width // head_dim
    seq_count = start_positions.shape[0]
    cache_len = kv_cache.shape[1]
    head_group = shard_count // KV_HEADS
    kv_index = shard_index // head_group
    frozen_weight_pair = w_keyvalue[0]
    row_float = hidden.astype(jnp.float32)
    normed = (
        row_float
        * lax.rsqrt(jnp.mean(row_float * row_float, axis=-1, keepdims=True) + norm_eps)
        * norm_gain
    ).astype(jnp.bfloat16)
    query_down, key_down, value_down, out_down, query_up, key_up, value_up, out_up = (
        lax.all_gather(a_query, "pool", axis=0, tiled=True),
        lax.all_gather(a_key, "pool", axis=0, tiled=True),
        lax.all_gather(a_value, "pool", axis=0, tiled=True),
        lax.all_gather(a_out, "pool", axis=0, tiled=True),
        lax.all_gather(b_query, "pool", axis=1, tiled=True),
        lax.all_gather(b_key, "pool", axis=1, tiled=True),
        lax.all_gather(b_value, "pool", axis=1, tiled=True),
        lax.all_gather(b_out, "pool", axis=1, tiled=True),
    )
    query_whole, key_whole, value_whole, key_upall, value_upall = (
        lax.all_gather(query_down, "tp", axis=0, tiled=True),
        lax.all_gather(key_down, "tp", axis=0, tiled=True),
        lax.all_gather(value_down, "tp", axis=0, tiled=True),
        lax.all_gather(key_up, "tp", axis=1, tiled=True),
        lax.all_gather(value_up, "tp", axis=1, tiled=True),
    )
    key_head = lax.dynamic_slice_in_dim(key_upall, kv_index * head_dim, head_dim, 1)
    value_head = lax.dynamic_slice_in_dim(value_upall, kv_index * head_dim, head_dim, 1)
    merged_query_weight = query_weight.astype(jnp.float32) + adapter_scale * jnp.dot(
        query_whole, query_up, preferred_element_type=jnp.float32
    )
    pair_difference = jnp.concatenate(
        [
            jnp.dot(key_whole, key_head, preferred_element_type=jnp.float32),
            jnp.dot(value_whole, value_head, preferred_element_type=jnp.float32),
        ],
        axis=1,
    )
    merged_weight_pair = frozen_weight_pair.astype(jnp.float32) + adapter_scale * pair_difference
    merged_input = jnp.concatenate([merged_query_weight, merged_weight_pair], axis=1)
    projected = highest_dot(
        lax.all_gather(normed, "tp", axis=0, tiled=True).astype(jnp.float32), merged_input
    )
    query = projected[:, :query_width]
    keys = projected[:, query_width : query_width + head_dim]
    values = projected[:, query_width + head_dim : query_width + 2 * head_dim]
    group_rows = projected.shape[0]
    draft_places = jnp.arange(VERIFY, dtype=jnp.int32)
    places = (start_positions[:, None] + draft_places[None, :]).reshape(group_rows)
    query = rotate(query.reshape(group_rows, heads_here, head_dim), places).astype(jnp.bfloat16)
    keys = rotate(keys.reshape(group_rows, 1, head_dim), places).astype(jnp.bfloat16)
    values = values.astype(jnp.bfloat16)
    query_seq = query.reshape(seq_count, VERIFY, heads_here, head_dim)
    key_seq = keys.reshape(seq_count, VERIFY, head_dim)
    value_seq = values.reshape(seq_count, VERIFY, head_dim)
    cached = kv_cache[:, :, 0, :]
    scale = 1.0 / math.sqrt(head_dim)
    cache_scores = (
        jnp.einsum(
            "sqhd,scd->shqc", query_seq, cached[..., :head_dim], preferred_element_type=jnp.float32
        )
        * scale
    )
    draft_scores = (
        jnp.einsum("sqhd,sjd->shqj", query_seq, key_seq, preferred_element_type=jnp.float32) * scale
    )
    allowed = (draft_places[None, None, :] <= draft_places[None, :, None]) & (
        draft_places[None, None, :] < draft_lengths[:, None, None]
    )
    draft_scores = jnp.where(allowed[:, None, :, :], draft_scores, -1e30)
    scores = jnp.concatenate([cache_scores, draft_scores], axis=-1)
    highest = jnp.max(scores, axis=-1, keepdims=True)
    powers = jnp.exp(scores - highest)
    weights = (powers / jnp.sum(powers, axis=-1, keepdims=True)).astype(jnp.bfloat16)
    mixed = jnp.einsum(
        "shqc,scd->sqhd",
        weights[..., :cache_len],
        cached[..., head_dim:],
        preferred_element_type=jnp.float32,
    )
    mixed = mixed + jnp.einsum(
        "shqj,sjd->sqhd", weights[..., cache_len:], value_seq, preferred_element_type=jnp.float32
    )
    active = (draft_places[None, :] < draft_lengths[:, None]).astype(jnp.float32)
    mixed = mixed * active[:, :, None, None]
    attended = mixed.reshape(group_rows, query_width).astype(jnp.bfloat16)
    out_upall = lax.all_gather(out_up, "tp", axis=1, tiled=True)
    merged_output_weight = output_weight.astype(jnp.float32) + adapter_scale * jnp.dot(
        out_down, out_upall, preferred_element_type=jnp.float32
    )
    branch = lax.psum_scatter(
        highest_dot(attended.astype(jnp.float32), merged_output_weight).astype(jnp.bfloat16),
        "tp",
        scatter_dimension=0,
        tiled=True,
    ).astype(jnp.float32)
    return (row_float + branch).astype(jnp.bfloat16)


def solution(mesh):
    in_specs = (
        P(("pool", "tp"), None),
        P(),
        P("pool"),
        P("pool"),
        P(None, "tp"),
        P("tp", None, None),
        P("tp", None),
        P("pool", None, "tp", None),
        P(("tp", "pool"), None),
        P(None, ("tp", "pool")),
        P(("tp", "pool"), None),
        P(None, ("tp", "pool")),
        P(("tp", "pool"), None),
        P(None, ("tp", "pool")),
        P(("tp", "pool"), None),
        P(None, ("tp", "pool")),
    )
    out_specs = P(("pool", "tp"), None)
    return jax.shard_map(shards, mesh=mesh, in_specs=in_specs, out_specs=out_specs, check_vma=False)
```

profile of v0, /device:TPU:64, one launch (start us, length us, event | category | flops | bytes accessed | tf_op | source)
XLA Modules:
  0.0 1018.0 jit_solution(2550070532810538157)
XLA Ops:
  6.5 17.6 %all_gather.55 = bf16[256,64]{1,0:T(8,128)(2,1)} all-gather(bf16[32,64]{1,0:T(8,128)(2,1)} %param.28), channel_id=1, replica_groups=mesh['pool'=8,'tp'=32] {'pool'}, dimensions={0}, use_global_device_ids=true | all-gather | bytes 36864 | tf_op jit(solution)/shard_map/all_gather | solution.py:73
  24.2 15.8 %all_gather.51 = bf16[256,64]{1,0:T(8,128)(2,1)} all-gather(bf16[32,64]{1,0:T(8,128)(2,1)} %param.26), channel_id=1, replica_groups=mesh['pool'=8,'tp'=32] {'pool'}, dimensions={0}, use_global_device_ids=true | all-gather | bytes 36864 | tf_op jit(solution)/shard_map/all_gather | solution.py:72
  40.1 15.9 %all_gather.46 = bf16[256,64]{1,0:T(8,128)(2,1)} all-gather(bf16[32,64]{1,0:T(8,128)(2,1)} %param.24), channel_id=1, replica_groups=mesh['pool'=8,'tp'=32] {'pool'}, dimensions={0}, use_global_device_ids=true | all-gather | bytes 36864 | tf_op jit(solution)/shard_map/all_gather | solution.py:71
  56.1 15.8 %all_gather.58 = bf16[64,256]{0,1:T(8,128)(2,1)} all-gather(bf16[64,32]{0,1:T(8,128)(2,1)} %param.31), channel_id=1, replica_groups=mesh['pool'=8,'tp'=32] {'pool'}, dimensions={1}, use_global_device_ids=true | all-gather | bytes 36864 | tf_op jit(solution)/shard_map/all_gather | solution.py:78
  72.0 1.1 fusion.12
  73.0 1.7 fusion.14
  74.8 6.4 copy.23
  81.2 6.5 copy.22
  87.9 10.1 all-gather.1
  97.9 11.1 %all-gather = bf16[8,4,64]{2,1,0:T(4,128)(2,1)S(1)} all-gather(bf16[1,4,64]{2,1,0:T(4,128)(2,1)S(1)} %bitcast.93), channel_id=1, replica_groups=mesh['pool'=8,'tp'=32] {'pool'}, dimensions={0}, use_global_device_ids=true | all-gather | bytes 4608 | tf_op jit(solution)/shard_map/all_gather | solution.py:76
  109.0 14.5 %all_gather.48 = bf16[64,256]{0,1:T(8,128)(2,1)S(1)} all-gather(bf16[64,32]{0,1:T(8,128)(2,1)S(1)} %copy-done.5), channel_id=1, replica_groups=mesh['pool'=8,'tp'=32] {'pool'}, dimensions={1}, use_global_device_ids=true | all-gather | bytes 36864 | tf_op jit(solution)/shard_map/all_gather | solution.py:75
  123.6 14.5 %all_gather.57 = bf16[256,64]{1,0:T(8,128)(2,1)S(1)} all-gather(bf16[32,64]{1,0:T(8,128)(2,1)S(1)} %copy-done.6), channel_id=1, replica_groups=mesh['pool'=8,'tp'=32] {'pool'}, dimensions={0}, use_global_device_ids=true | all-gather | bytes 36864 | tf_op jit(solution)/shard_map/all_gather | solution.py:74
  138.1 82.4 %all_gather.54 = bf16[64,1024]{0,1:T(8,128)(2,1)S(1)} all-gather(bf16[64,32]{0,1:T(8,128)(2,1)S(1)} %bitcast.91), channel_id=1, replica_groups=mesh['pool'=8,'tp'=32] {'tp'}, dimensions={1}, use_global_device_ids=true | all-gather | bytes 135168 | tf_op jit(solution)/shard_map/all_gather | solution.py:85
  220.5 76.9 %all_gather.50 = bf16[64,1024]{0,1:T(8,128)(2,1)S(1)} all-gather(bf16[64,32]{0,1:T(8,128)(2,1)S(1)} %bitcast.90), channel_id=1, replica_groups=mesh['pool'=8,'tp'=32] {'tp'}, dimensions={1}, use_global_device_ids=true | all-gather | bytes 135168 | tf_op jit(solution)/shard_map/all_gather | solution.py:84
  297.9 4.3 convolution_bitcast_fusion
  302.2 35.2 %all-gather.12.cloned.1.call-done = bf16[8192,64]{1,0:T(8,128)(2,1)} async-done(((bf16[256,64]{1,0:T(8,128)(2,1)}), bf16[8192,64]{1,0:T(8,128)(2,1)}) %all-gather.12.cloned.1.call-update) | async-done | bytes 1048592 | tf_op jit(solution)/shard_map/all_gather | solution.py:82
  337.4 4.3 convolution_bitcast_fusion.1
  341.7 152.7 %all-gather.10.cloned.1.call-done = bf16[8192,64]{1,0:T(8,128)(2,1)} async-done(((bf16[256,64]{1,0:T(8,128)(2,1)}), bf16[8192,64]{1,0:T(8,128)(2,1)}) %all-gather.10.cloned.1.call-update) | async-done | bytes 1048592 | tf_op jit(solution)/shard_map/all_gather | solution.py:81
  494.4 7.3 convolution_add_fusion.1
  501.7 149.3 %all-gather.16.cloned.1.call-done = bf16[64,8192]{0,1:T(8,128)(2,1)} async-done(((bf16[64,256]{0,1:T(8,128)(2,1)}), bf16[64,8192]{0,1:T(8,128)(2,1)}) %all-gather.16.cloned.1.call-update) | async-done | bytes 1048592 | tf_op jit(solution)/shard_map/all_gather | solution.py:147
  651.0 8.5 convolution_add_fusion
  659.5 1.0 copy-done.2
  660.5 3.8 maximum_add_fusion
  664.4 147.7 %all-gather.8.cloned.1.call-done = bf16[256,8192]{1,0:T(8,128)(2,1)} async-done(((bf16[8,8192]{1,0:T(8,128)(2,1)}), bf16[256,8192]{1,0:T(8,128)(2,1)}) %all-gather.8.cloned.1.call-update) | async-done | bytes 4194320 | tf_op jit(solution)/shard_map/all_gather | solution.py:102
  812.0 12.3 %fusion = f32[256,512]{1,0:T(8,128)S(1)} fusion(bf16[256,8192]{1,0:T(8,128)(2,1)} %all-gather.8.cloned.1.call-done, f32[8192,256]{0,1:T(8,128)} %maximum_add_fusion, f32[8192,256]{0,1:T(8,128)} %convolution_add_fusion.1), kind=kOutput, calls=%fused_computation | convolution fusion | flops 12889096192 | bytes 21495808 | tf_op jit(solution)/shard_map/dot_general | solution.py:33
  825.1 0.6 fusion.22
  825.7 0.4 fusion.38
  826.1 0.4 fusion.39
  826.5 0.3 fusion.11
  827.6 11.8 %convolution_convert_fusion = bf16[256,8192]{1,0:T(8,128)(2,1)} fusion(f32[256,8192]{1,0:T(8,128)} %convolution_add_fusion, bf16[32,8,2,128]{3,2,1,0:T(2,128)(2,1)S(1)} %bitcast.84), kind=kOutput, calls=%fused_computation.6 | convolution fusion | flops 6444548096 | bytes 12713984 | tf_op jit(solution)/shard_map/dot_general | solution.py:33
  839.4 170.2 %reduce-scatter.2.cloned.1.call-done = bf16[8,8192]{1,0:T(8,128)(2,1)} async-done(((bf16[256,8192]{1,0:T(8,128)(2,1)}), bf16[8,8192]{1,0:T(8,128)(2,1)}) %reduce-scatter.2.cloned.1.call-update) | async-done | bytes 131088 | tf_op jit(solution)/shard_map/reduce_scatter | solution.py:151
  1009.5 1.6 fusion.15
  (56 shorter events, 2.5 us)
Async XLA Ops:
  6.5 291.3 %all-gather.14.cloned.1.call-start = ((), (), s32[]{:S(2)}) async-start(), calls=%async_computation.4 | async-start | bytes 2162688 | tf_op jit(solution)/shard_map/all_gather | solution.py:83
  24.2 313.2 %all-gather.12.cloned.1.call-start = ((), (), s32[]{:S(2)}) async-start(), calls=%async_computation.3 | async-start | bytes 2162688 | tf_op jit(solution)/shard_map/all_gather | solution.py:82
  40.1 454.3 %all-gather.10.cloned.1.call-start = ((), (), s32[]{:S(2)}) async-start(), calls=%async_computation.2 | async-start | bytes 2162688 | tf_op jit(solution)/shard_map/all_gather | solution.py:81
  56.0 595.0 %all-gather.16.cloned.1.call-start = ((), (), s32[]{:S(2)}) async-start(), calls=%async_computation.5 | async-start | bytes 2162688 | tf_op jit(solution)/shard_map/all_gather | solution.py:147
  71.9 740.1 %all-gather.8.cloned.1.call-start = ((), (), s32[]{:S(2)}) async-start(), calls=%async_computation.1 | async-start | bytes 4325376 | tf_op jit(solution)/shard_map/all_gather | solution.py:102
  74.7 934.8 %reduce-scatter.2.cloned.1.call-start = ((), (), s32[]{:S(2)}) async-start(), calls=%async_computation.6 | async-start | bytes 4325376 | tf_op jit(solution)/shard_map/reduce_scatter | solution.py:151
  81.2 6.5 copy-start.9
  81.2 6.7 copy-start.7
  81.2 16.7 %copy-start.8 = (bf16[64,4]{0,1:T(4,128)(2,1)S(1)}, bf16[64,4]{0,1:T(4,128)(2,1)}, u32[]{:S(2)}) copy-start(bf16[64,4]{0,1:T(4,128)(2,1)} %param.27) | copy-start | bytes 1540
  81.2 27.8 %copy-start.5 = (bf16[64,32]{0,1:T(8,128)(2,1)S(1)}, bf16[64,32]{0,1:T(8,128)(2,1)}, u32[]{:S(2)}) copy-start(bf16[64,32]{0,1:T(8,128)(2,1)} %param.25) | copy-start | bytes 12292
  81.2 42.4 %copy-start.6 = (bf16[32,64]{1,0:T(8,128)(2,1)S(1)}, bf16[32,64]{1,0:T(8,128)(2,1)}, u32[]{:S(2)}) copy-start(bf16[32,64]{1,0:T(8,128)(2,1)} %param.30) | copy-start | bytes 12292
  81.2 216.2 %copy-start.10 = (s32[4]{0:T(128)S(1)}, s32[4]{0:T(128)}, u32[]{:S(2)}) copy-start(s32[4]{0:T(128)} %param.19) | copy-start | bytes 52
  651.0 8.5 copy-start
  651.0 8.5 copy-start.1
  651.0 9.5 copy-start.2
  664.4 161.3 %copy-start.4 = (bf16[4,256,1,256]{3,1,2,0:T(8,128)(2,1)S(1)}, bf16[4,256,1,256]{3,1,2,0:T(8,128)(2,1)}, u32[]{:S(2)}) copy-start(bf16[4,256,1,256]{3,1,2,0:T(8,128)(2,1)} %param.23) | copy-start | bytes 1572868
  839.3 170.2 %copy-start.3 = (bf16[8,8192]{1,0:T(8,128)(2,1)S(1)}, bf16[8,8192]{1,0:T(8,128)(2,1)}, u32[]{:S(2)}) copy-start(bf16[8,8192]{1,0:T(8,128)(2,1)} %param.16) | copy-start | bytes 393220
Sparse Core Ops, SparseCore 0:
  24.3 156.1 all-gather.13
  182.3 155.0 all-gather.11
  339.2 155.1 all-gather.9
  496.0 154.9 all-gather.15
  652.6 159.3 all-gather.7
  839.5 170.0 reduce-scatter.1
where the time goes:
time: 1020 us
  waiting for transfers between devices  655 us (64%)
  blocking collectives  275 us (27%)
  matrix products  49.5 us (5%)
  local copies, waits for them, and re-layouts  14.9 us (1%)
  between operations  13.7 us (1%)
    reduce_scatter x1, waiting for transfers between devices, shards(): lax.psum_scatter(highest_dot(attended.astype(jnp.float32), merged_output_...  170 us
    all_gather x1, waiting for transfers between devices, shards(): lax.all_gather(query_down, 'tp', axis=0, tiled=True)  153 us
    all_gather x1, waiting for transfers between devices, shards(): out_upall = lax.all_gather(out_up, 'tp', axis=1, tiled=True)  149 us
    all_gather x1, waiting for transfers between devices, shards(): lax.all_gather(normed, 'tp', axis=0, tiled=True).astype(jnp.float32)  148 us
    all_gather x1, blocking collectives, shards(): lax.all_gather(value_up, 'tp', axis=1, tiled=True)  82.4 us
    all_gather x1, blocking collectives, shards(): lax.all_gather(key_up, 'tp', axis=1, tiled=True)  76.9 us
    all_gather x1, waiting for transfers between devices, shards(): lax.all_gather(key_down, 'tp', axis=0, tiled=True)  35.2 us
    dot_general x2, matrix products, highest_dot(): return jnp.dot(left, right, precision=lax.Precision.HIGHEST)  24 us
  transfers between devices with their start and end apart: 6, of which 5 were waited for; matrix products, arithmetic and copies ran while one was open for 4% of the time, Pallas kernels for 0%

commit v1 on v0

v1 whole, which is shorter than its diff:
```python
import math

import jax
import jax.numpy as jnp
from jax import lax
from jax.sharding import Mesh, PartitionSpec as P

VERIFY = 64
HEAD_DIM = 128

adapter_scale = 1.0
rope_base = 1000000.0
norm_eps = 1e-06

AXES = ("zh", "core", "x", "zl", "y")
TP = ("x", "zl", "y")
POOL = ("zh", "core")


def rotate(values, places):
    half_dim = values.shape[-1] // 2
    freqs = jnp.exp(
        jnp.arange(half_dim, dtype=jnp.float32) * (-2.0 * math.log(rope_base) / values.shape[-1])
    )
    angles = places.astype(jnp.float32)[:, None] * freqs[None, :]
    cosine = jnp.cos(angles)[:, None, :]
    sine = jnp.sin(angles)[:, None, :]
    first = values[..., :half_dim]
    second = values[..., half_dim:]
    return jnp.concatenate(
        [first * cosine - second * sine, second * cosine + first * sine], axis=-1
    )


def dot32(left, right):
    return jnp.dot(left, right, preferred_element_type=jnp.float32)


def spread(block, axes):
    count = lax.axis_size(axes)
    return lax.all_to_all(jnp.broadcast_to(block[None], (count,) + block.shape), axes, 0, 0)


def shards(
    hidden,
    norm_gain,
    start_positions,
    draft_lengths,
    query_weight,
    w_keyvalue,
    output_weight,
    kv_cache,
    a_query,
    b_query,
    a_key,
    b_key,
    a_value,
    b_value,
    a_out,
    b_out,
):
    shard_index = lax.axis_index(TP)
    head_dim = w_keyvalue.shape[2] // 2
    query_width = query_weight.shape[1]
    heads_here = query_width // head_dim
    seq_count = start_positions.shape[0]
    cache_len = kv_cache.shape[1]
    row_float = hidden.astype(jnp.float32)
    normed = (
        row_float
        * lax.rsqrt(jnp.mean(row_float * row_float, axis=-1, keepdims=True) + norm_eps)
        * norm_gain
    ).astype(jnp.bfloat16)

    packed = jnp.concatenate(
        [
            jnp.concatenate([a_query, a_key], axis=1),
            jnp.concatenate([a_value, a_out], axis=1),
            jnp.concatenate([b_query.T, b_out.T], axis=1),
            jnp.concatenate([b_key.T, b_value.T], axis=1),
        ],
        axis=0,
    )
    pooled = spread(packed, POOL)
    down_first = pooled[:, 0:32].reshape(256, 128)
    down_second = pooled[:, 32:64].reshape(256, 128)
    up_wide = pooled[:, 64:96].reshape(256, 128)
    up_narrow = pooled[:, 96:100].reshape(32, 128)
    down_in = jnp.concatenate([down_first, down_second[:, :64]], axis=1)
    down_out = down_second[:, 64:]
    query_up = up_wide[:, :64]
    narrow = spread(up_narrow, "y").reshape(128, 128)
    key_up = narrow[:, :64]
    value_up = narrow[:, 64:]
    out_up = spread(up_wide[:, 64:], TP).reshape(8192, 64)

    rows = spread(normed, TP).reshape(256, 8192)
    mine = lax.dynamic_slice_in_dim(rows, shard_index * 256, 256, 1)
    inner = dot32(mine, down_in).astype(jnp.bfloat16).reshape(32, 8, 192)
    inner = lax.all_to_all(inner, TP, 0, 0).astype(jnp.float32).sum(0).astype(jnp.bfloat16)
    inner = spread(inner, TP).reshape(256, 192)

    def up(inner, factor):
        return lax.dot_general(
            inner, factor, (((1,), (1,)), ((), ())), preferred_element_type=jnp.float32
        )

    query = dot32(rows, query_weight) + adapter_scale * up(inner[:, :64], query_up)
    pair = dot32(rows, w_keyvalue[0])
    keys = pair[:, :head_dim] + adapter_scale * up(inner[:, 64:128], key_up)
    values = pair[:, head_dim:] + adapter_scale * up(inner[:, 128:], value_up)
    group_rows = 256
    draft_places = jnp.arange(VERIFY, dtype=jnp.int32)
    places = (start_positions[:, None] + draft_places[None, :]).reshape(group_rows)
    query = rotate(query.reshape(group_rows, heads_here, head_dim), places).astype(jnp.bfloat16)
    keys = rotate(keys.reshape(group_rows, 1, head_dim), places).astype(jnp.bfloat16)
    values = values.astype(jnp.bfloat16)
    query_seq = query.reshape(seq_count, VERIFY, heads_here, head_dim)
    key_seq = keys.reshape(seq_count, VERIFY, head_dim)
    value_seq = values.reshape(seq_count, VERIFY, head_dim)
    cached = kv_cache[:, :, 0, :]
    scale = 1.0 / math.sqrt(head_dim)
    cache_scores = (
        jnp.einsum(
            "sqhd,scd->shqc", query_seq, cached[..., :head_dim], preferred_element_type=jnp.float32
        )
        * scale
    )
    draft_scores = (
        jnp.einsum("sqhd,sjd->shqj", query_seq, key_seq, preferred_element_type=jnp.float32) * scale
    )
    allowed = (draft_places[None, None, :] <= draft_places[None, :, None]) & (
        draft_places[None, None, :] < draft_lengths[:, None, None]
    )
    draft_scores = jnp.where(allowed[:, None, :, :], draft_scores, -1e30)
    scores = jnp.concatenate([cache_scores, draft_scores], axis=-1)
    highest = jnp.max(scores, axis=-1, keepdims=True)
    powers = jnp.exp(scores - highest)
    weights = (powers / jnp.sum(powers, axis=-1, keepdims=True)).astype(jnp.bfloat16)
    mixed = jnp.einsum(
        "shqc,scd->sqhd",
        weights[..., :cache_len],
        cached[..., head_dim:],
        preferred_element_type=jnp.float32,
    )
    mixed = mixed + jnp.einsum(
        "shqj,sjd->sqhd", weights[..., cache_len:], value_seq, preferred_element_type=jnp.float32
    )
    active = (draft_places[None, :] < draft_lengths[:, None]).astype(jnp.float32)
    mixed = mixed * active[:, :, None, None]
    attended = mixed.reshape(group_rows, query_width).astype(jnp.bfloat16)

    out_inner = dot32(attended, down_out).astype(jnp.bfloat16)
    partial = (dot32(attended, output_weight) + adapter_scale * up(out_inner, out_up)).astype(
        jnp.bfloat16
    )
    partial = lax.all_to_all(partial.reshape(32, 8, 8192), TP, 0, 0)
    branch = partial.astype(jnp.float32).sum(0)
    return (row_float + branch).astype(jnp.bfloat16)


def solution(mesh):
    fine = Mesh(mesh.devices.reshape(4, 2, 4, 2, 4), AXES)
    both = ("x", "zl", "y", "zh", "core")
    in_specs = (
        P(AXES, None),
        P(),
        P(POOL),
        P(POOL),
        P(None, TP),
        P(TP, None, None),
        P(TP, None),
        P(POOL, None, TP, None),
        P(both, None),
        P(None, both),
        P(both, None),
        P(None, both),
        P(both, None),
        P(None, both),
        P(both, None),
        P(None, both),
    )
    out_specs = P(AXES, None)
    return jax.shard_map(shards, mesh=fine, in_specs=in_specs, out_specs=out_specs, check_vma=False)
```

time: 1020 us -> 218 us (0.21)
  waiting for transfers between devices: 655 us -> 89.8 us
  blocking collectives: 275 us -> 53.8 us
  starting transfers between devices: 0.21 us -> 33.8 us
  matrix products: 49.5 us -> 24.8 us
  between operations: 13.7 us -> 0.31 us
    all_gather x5 -> x0, waiting for transfers between devices: 485 us -> none  [the longest x1 153 us: shards(): lax.all_gather(query_down, 'tp', axis=0, tiled=True)]
    all_gather x10 -> x0, blocking collectives: 275 us -> none  [the longest x1 82.4 us: shards(): lax.all_gather(value_up, 'tp', axis=1, tiled=True)]
    reduce_scatter x1 -> x0, waiting for transfers between devices: 170 us -> none  [shards(): lax.psum_scatter(highest_dot(attended.astype(jnp.float32), merged_output_...]
    all_to_all x0 -> x6, waiting for transfers between devices: none -> 89.8 us  [the longest x5 81.2 us: spread(): lax.all_to_all(jnp.broadcast_to(block[None], (count,) + block.shape), axe...]
    all_to_all x0 -> x1, blocking collectives: none -> 53.8 us  [shards(): partial = lax.all_to_all(partial.reshape(32, 8, 8192), TP, 0, 0)]
    all_to_all x0 -> x6, starting transfers between devices: none -> 33.8 us  [the longest x5 29 us: spread(): lax.all_to_all(jnp.broadcast_to(block[None], (count,) + block.shape), axe...]
    dot_general x6 -> x8, matrix products: 48.4 us -> 23.6 us  [the longest x4 16.1 us: dot32(): return jnp.dot(left, right, preferred_element_type=jnp.float32)]
    unnamed x24 -> x10, local copies, waits for them, and re-layouts: 14 us -> 0.66 us
  transfers between devices with their start and end apart: 6 -> 6, of which waited for: 5 -> 6; matrix products, arithmetic and copies ran while one was open for 4% -> 7% of each run, Pallas kernels for 0% -> 0%
where the time goes in v1:
time: 218 us; the launch traced here: 216 us
  waiting for transfers between devices  89.8 us (41%)
  blocking collectives  53.8 us (25%)
  starting transfers between devices  33.8 us (16%)
  matrix products  24.8 us (11%)
  local copies, waits for them, and re-layouts  8.3 us (4%)
  other arithmetic  5.69 us (3%)
    all_to_all x5, waiting for transfers between devices, spread(): lax.all_to_all(jnp.broadcast_to(block[None], (count,) + block.shape), axe...  81.2 us
    all_to_all x1, blocking collectives, shards(): partial = lax.all_to_all(partial.reshape(32, 8, 8192), TP, 0, 0)  53.8 us
    all_to_all x5, starting transfers between devices, spread(): lax.all_to_all(jnp.broadcast_to(block[None], (count,) + block.shape), axe...  29 us
    dot_general x4, matrix products, dot32(): return jnp.dot(left, right, preferred_element_type=jnp.float32)  16.1 us
    all_to_all x1, waiting for transfers between devices, shards(): lax.all_to_all(inner, TP, 0, 0).astype(jnp.float32).sum(0)  8.6 us
    dot_general x4, matrix products, up(): lax.dot_general(inner, factor, (((1,), (1,)), ((), ())), preferred_elemen...  7.57 us
    broadcast_in_dim x5, local copies, waits for them, and re-layouts, spread(): jnp.broadcast_to(block[None], (count,) + block.shape)  5.52 us
    all_to_all x1, starting transfers between devices, shards(): lax.all_to_all(inner, TP, 0, 0).astype(jnp.float32).sum(0)  4.78 us
  transfers between devices with their start and end apart: 6, of which 6 were waited for; matrix products, arithmetic and copies ran while one was open for 7% of the time, Pallas kernels for 0%

profile of v1, /device:TPU:64, one launch (start us, length us, event | category | flops | bytes accessed | tf_op | source)
XLA Modules:
  0.0 216.4 jit_solution(12806221806302975820)
XLA Ops:
  0.0 0.9 maximum_maximum_fusion
  0.9 0.7 broadcast_in_dim.21
  1.6 8.1 %all-to-all-start.1 = ((bf16[8,100,128]{2,1,0:T(8,128)(2,1)}), bf16[8,100,128]{2,1,0:T(8,128)(2,1)S(1)}, u32[]{:S(2)}, u32[]{:S(2)}) async-start(bf16[8,100,128]{2,1,0:T(8,128)(2,1)} %broadcast_in_dim.21), calls=%async_computation.1 | async-start | bytes 425984 | tf_op jit(solution)/shard_map/all_to_all | solution.py:41
  9.7 1.1 fusion.14
  10.8 1.0 fusion.16
  11.8 7.2 %all-to-all-done.1 = bf16[8,100,128]{2,1,0:T(8,128)(2,1)S(1)} async-done(((bf16[8,100,128]{2,1,0:T(8,128)(2,1)}), bf16[8,100,128]{2,1,0:T(8,128)(2,1)S(1)}, u32[]{:S(2)}, u32[]{:S(2)}) %all-to-all-start.1) | async-done | bytes 204832 | tf_op jit(solution)/shard_map/all_to_all | solution.py:41
  19.0 2.4 %broadcast_in_dim.20 = bf16[32,8,8192]{2,1,0:T(8,128)(2,1)} broadcast(bf16[8,8192]{1,0:T(8,128)(2,1)S(1)} %fusion.16), dimensions={1,2} | broadcast | bytes 4325376 | tf_op jit(solution)/shard_map/broadcast_in_dim | solution.py:41
  21.5 7.6 %all-to-all-start = ((bf16[32,8,8192]{2,1,0:T(8,128)(2,1)}), bf16[32,8,8192]{2,1,0:T(8,128)(2,1)}, u32[]{:S(2)}, u32[]{:S(2)}) async-start(bf16[32,8,8192]{2,1,0:T(8,128)(2,1)} %broadcast_in_dim.20), calls=%async_computation | async-start | bytes 8388608 | tf_op jit(solution)/shard_map/all_to_all | solution.py:41
  29.3 57.9 %all-to-all-done = bf16[32,8,8192]{2,1,0:T(8,128)(2,1)} async-done(((bf16[32,8,8192]{2,1,0:T(8,128)(2,1)}), bf16[32,8,8192]{2,1,0:T(8,128)(2,1)}, u32[]{:S(2)}, u32[]{:S(2)}) %all-to-all-start) | async-done | bytes 4194336 | tf_op jit(solution)/shard_map/all_to_all | solution.py:41
  87.1 1.1 broadcast_in_dim.27
  88.2 4.2 %all-to-all-start.5 = ((bf16[32,256,64]{1,2,0:T(8,128)(2,1)}), bf16[32,256,64]{1,2,0:T(8,128)(2,1)S(1)}, u32[]{:S(2)}, u32[]{:S(2)}) async-start(bf16[32,256,64]{1,2,0:T(8,128)(2,1)} %broadcast_in_dim.27), calls=%async_computation.5 | async-start | bytes 2097152 | tf_op jit(solution)/shard_map/all_to_all | solution.py:41
  93.0 1.1 convolution_convert_fusion
  94.2 0.8 copy.39
  95.0 12.5 %all-to-all-done.5 = bf16[32,256,64]{1,2,0:T(8,128)(2,1)S(1)} async-done(((bf16[32,256,64]{1,2,0:T(8,128)(2,1)}), bf16[32,256,64]{1,2,0:T(8,128)(2,1)S(1)}, u32[]{:S(2)}, u32[]{:S(2)}) %all-to-all-start.5) | async-done | bytes 1048608 | tf_op jit(solution)/shard_map/all_to_all | solution.py:41
  107.5 4.8 %all-to-all-start.2 = ((bf16[32,8,192]{2,1,0:T(8,128)(2,1)}), bf16[32,8,192]{2,1,0:T(8,128)(2,1)S(1)}, u32[]{:S(2)}, u32[]{:S(2)}) async-start(bf16[32,8,192]{2,1,0:T(8,128)(2,1)} %bitcast.7), calls=%async_computation.2 | async-start | bytes 262144 | tf_op jit(solution)/shard_map/all_to_all | solution.py:100
  112.4 8.6 %all-to-all-done.2 = bf16[32,8,192]{2,1,0:T(8,128)(2,1)S(1)} async-done(((bf16[32,8,192]{2,1,0:T(8,128)(2,1)}), bf16[32,8,192]{2,1,0:T(8,128)(2,1)S(1)}, u32[]{:S(2)}, u32[]{:S(2)}) %all-to-all-start.2) | async-done | bytes 98336 | tf_op jit(solution)/shard_map/all_to_all | solution.py:100
  121.0 0.6 broadcast_in_dim.25
  121.6 3.3 %all-to-all-start.4 = ((bf16[4,32,128]{2,1,0:T(8,128)(2,1)}), bf16[4,32,128]{2,1,0:T(8,128)(2,1)S(1)}, u32[]{:S(2)}, u32[]{:S(2)}) async-start(bf16[4,32,128]{2,1,0:T(8,128)(2,1)} %broadcast_in_dim.25), calls=%async_computation.4 | async-start | bytes 65536 | tf_op jit(solution)/shard_map/all_to_all | solution.py:41
  124.9 5.2 %fusion.2 = f32[256,256]{0,1:T(8,128)S(1)} fusion(bf16[1,8192,256]{2,1,0:T(8,128)(2,1)} %param.21, bf16[32,8,8192]{2,1,0:T(8,128)(2,1)} %all-to-all-done), kind=kOutput, calls=%fused_computation.4 | convolution fusion | flops 1073741824 | bytes 8650752 | tf_op jit(solution)/shard_map/dot_general | solution.py:36
  130.3 0.7 broadcast_in_dim.22
  130.9 5.8 %all-to-all-start.3 = ((bf16[32,8,192]{2,1,0:T(8,128)(2,1)}), bf16[32,8,192]{2,1,0:T(8,128)(2,1)S(1)}, u32[]{:S(2)}, u32[]{:S(2)}) async-start(bf16[32,8,192]{2,1,0:T(8,128)(2,1)} %broadcast_in_dim.22), calls=%async_computation.3 | async-start | bytes 262144 | tf_op jit(solution)/shard_map/all_to_all | solution.py:41
  136.8 5.2 %fusion.54 = f32[256,256]{0,1:T(8,128)S(1)} fusion(bf16[8192,256]{1,0:T(8,128)(2,1)} %param.20, bf16[32,8,8192]{2,1,0:T(8,128)(2,1)} %all-to-all-done), kind=kOutput, calls=%fused_computation.84 | convolution fusion | flops 1073741824 | bytes 8650752 | tf_op jit(solution)/shard_map/dot_general | solution.py:36
  142.0 3.5 %all-to-all-done.3 = bf16[32,8,192]{2,1,0:T(8,128)(2,1)S(1)} async-done(((bf16[32,8,192]{2,1,0:T(8,128)(2,1)}), bf16[32,8,192]{2,1,0:T(8,128)(2,1)S(1)}, u32[]{:S(2)}, u32[]{:S(2)}) %all-to-all-start.3) | async-done | bytes 98336 | tf_op jit(solution)/shard_map/all_to_all | solution.py:41
  146.4 0.3 fusion.36
  147.4 0.4 fusion.58
  147.8 0.4 fusion.59
  149.6 4.5 %fusion.21 = f32[256,8192]{1,0:T(8,128)} fusion(bf16[256,8192]{1,0:T(8,128)(2,1)S(1)} %copy-done, bf16[32,8,2,128]{3,2,1,0:T(2,128)(2,1)S(1)} %bitcast.88), kind=kOutput, calls=%fused_computation.38 | convolution fusion | flops 1073741824 | bytes 12713984 | tf_op jit(solution)/shard_map/dot_general | solution.py:36
  154.1 6.9 %fusion.1 = bf16[32,8,8192]{2,1,0:T(8,128)(2,1)} fusion(f32[256,8192]{1,0:T(8,128)} %fusion.21, bf16[8192,64]{0,1:T(8,128)(2,1)S(1)} %bitcast.87, bf16[32,8,2,128]{3,2,1,0:T(2,128)(2,1)S(1)} %bitcast.89, bf16[256,128]{1,0:T(8,128)(2,1)S(1)} %bitcast.95), kind=kOutput, calls=%fused_computation.2 | convolution fusion | flops 281034752 | bytes 13828096 | tf_op jit(solution)/shard_map/dot_general | solution.py:104
  161.0 53.8 %all_to_all.35 = bf16[32,8,8192]{2,1,0:T(8,128)(2,1)S(1)} all-to-all(bf16[32,8,8192]{2,1,0:T(8,128)(2,1)} %fusion.1), channel_id=1, replica_groups=mesh['zh'=4,'core'=2,'x'=4,'zl'=2,'y'=4] {'x','zl','y'}, dimensions={0} | all-to-all | bytes 8388608 | tf_op jit(solution)/shard_map/all_to_all | solution.py:157
  214.8 0.6 convert_reduce_fusion
  215.4 0.3 copy-done.1
  215.7 0.7 fusion.17
  (41 shorter events, 4.0 us)
Async XLA Ops:
  1.6 17.4 %all-to-all-start.1 = ((bf16[8,100,128]{2,1,0:T(8,128)(2,1)}), bf16[8,100,128]{2,1,0:T(8,128)(2,1)S(1)}, u32[]{:S(2)}, u32[]{:S(2)}) async-start(bf16[8,100,128]{2,1,0:T(8,128)(2,1)} %broadcast_in_dim.21), calls=%async_computation.1 | async-start | bytes 425984 | tf_op jit(solution)/shard_map/all_to_all | solution.py:41
  21.5 71.0 %copy-start.3 = (s32[4]{0:T(128)S(1)}, s32[4]{0:T(128)}, u32[]{:S(2)}) copy-start(s32[4]{0:T(128)} %param.18) | copy-start | bytes 52
  21.5 71.2 %copy-start.4 = (s32[4]{0:T(128)S(1)}, s32[4]{0:T(128)}, u32[]{:S(2)}) copy-start(s32[4]{0:T(128)} %param.19) | copy-start | bytes 52
  21.5 65.7 %all-to-all-start = ((bf16[32,8,8192]{2,1,0:T(8,128)(2,1)}), bf16[32,8,8192]{2,1,0:T(8,128)(2,1)}, u32[]{:S(2)}, u32[]{:S(2)}) async-start(bf16[32,8,8192]{2,1,0:T(8,128)(2,1)} %broadcast_in_dim.20), calls=%async_computation | async-start | bytes 8388608 | tf_op jit(solution)/shard_map/all_to_all | solution.py:41
  88.2 19.3 %all-to-all-start.5 = ((bf16[32,256,64]{1,2,0:T(8,128)(2,1)}), bf16[32,256,64]{1,2,0:T(8,128)(2,1)S(1)}, u32[]{:S(2)}, u32[]{:S(2)}) async-start(bf16[32,256,64]{1,2,0:T(8,128)(2,1)} %broadcast_in_dim.27), calls=%async_computation.5 | async-start | bytes 2097152 | tf_op jit(solution)/shard_map/all_to_all | solution.py:41
  107.5 13.5 %all-to-all-start.2 = ((bf16[32,8,192]{2,1,0:T(8,128)(2,1)}), bf16[32,8,192]{2,1,0:T(8,128)(2,1)S(1)}, u32[]{:S(2)}, u32[]{:S(2)}) async-start(bf16[32,8,192]{2,1,0:T(8,128)(2,1)} %bitcast.7), calls=%async_computation.2 | async-start | bytes 262144 | tf_op jit(solution)/shard_map/all_to_all | solution.py:100
  121.6 8.7 %all-to-all-start.4 = ((bf16[4,32,128]{2,1,0:T(8,128)(2,1)}), bf16[4,32,128]{2,1,0:T(8,128)(2,1)S(1)}, u32[]{:S(2)}, u32[]{:S(2)}) async-start(bf16[4,32,128]{2,1,0:T(8,128)(2,1)} %broadcast_in_dim.25), calls=%async_computation.4 | async-start | bytes 65536 | tf_op jit(solution)/shard_map/all_to_all | solution.py:41
  130.9 14.5 %all-to-all-start.3 = ((bf16[32,8,192]{2,1,0:T(8,128)(2,1)}), bf16[32,8,192]{2,1,0:T(8,128)(2,1)S(1)}, u32[]{:S(2)}, u32[]{:S(2)}) async-start(bf16[32,8,192]{2,1,0:T(8,128)(2,1)} %broadcast_in_dim.22), calls=%async_computation.3 | async-start | bytes 262144 | tf_op jit(solution)/shard_map/all_to_all | solution.py:41
  136.7 10.7 %copy-start.2 = (bf16[4,256,1,256]{3,1,2,0:T(8,128)(2,1)S(1)}, bf16[4,256,1,256]{3,1,2,0:T(8,128)(2,1)}, u32[]{:S(2)}) copy-start(bf16[4,256,1,256]{3,1,2,0:T(8,128)(2,1)} %param.23) | copy-start | bytes 1572868
  147.4 2.2 %copy-start = (bf16[256,8192]{1,0:T(8,128)(2,1)S(1)}, bf16[256,8192]{1,0:T(8,128)(2,1)}, u32[]{:S(2)}) copy-start(bf16[256,8192]{1,0:T(8,128)(2,1)} %param.22) | copy-start | bytes 12582916
  214.8 0.9 copy-start.1
